TPU v7x, 32 devices: a whole 2x2x4 slice. The times are simulated.
32 devices in a mesh: group: 2 (over x), expert: 4 (over z), hid: 4 (over y, core).
Axes of the slice: x: 2, y: 2, z: 4, core: 2. Of those that a mesh axis runs over, the one named last changes fastest.
Arguments:
- tokens: bfloat16 [256, 4096], P(('group', 'expert', 'hid')), may hold values from -6 to 6
- expert_ids: int32 [256, 2], P(('group', 'expert', 'hid')), may hold values from 0 to 7, all different within a row; in each aligned block of 8 rows (0 to 7, 8 to 15, ...) at most 4 rows name the same one
- gate_numer: int32 [256, 2], P(('group', 'expert', 'hid')), may hold values from 8 to 64
- gate_weight: bfloat16 [8, 4096, 14336], P('group', None, ('expert', 'hid')), may hold values from -0.09375 to 0.09375
- up_weight: bfloat16 [8, 4096, 14336], P('group', None, ('expert', 'hid')), may hold values from -0.09375 to 0.09375
- down_weight: bfloat16 [8, 14336, 4096], P('group', ('expert', 'hid')), may hold values from -0.046875 to 0.046875
Outputs:
- mixed: bfloat16 [256, 4096], P(('group', 'expert', 'hid'))
Inputs may be any that keep to these rules, and one draw needn't show every extreme that they name: `expert_ids`: A token's 2 ids differ. Within the rows of one device (aligned blocks of 8 rows) no expert is named more than 4 times, and in every draw some block names some expert exactly 4 times.
All inputs are finite; a program needn't handle non-finite values.
Results may differ from a plain program's by a relative error of at most 0.018.
Values may be sent and summed in bfloat16 or wider, within the bound.
A program may use at most 192 MiB of HBM per device.

v0:
```python
import jax
import jax.numpy as jnp
from jax import lax
from jax.sharding import PartitionSpec as P

TOPK = 2
CAP = 4


def expert_block(block, w_gate, w_up, w_down):
    local = w_gate.shape[0]
    grid = block.reshape(-1, local, CAP, block.shape[-1])
    gate = jnp.einsum("mlcd,ldf->mlcf", grid, w_gate, preferred_element_type=jnp.float32)
    upper = jnp.einsum("mlcd,ldf->mlcf", grid, w_up, preferred_element_type=jnp.float32)
    hidden = (jax.nn.silu(gate) * upper).astype(jnp.bfloat16)
    output = jnp.einsum("mlcf,lfd->mlcd", hidden, w_down, preferred_element_type=jnp.float32)
    return output.reshape(block.shape)


def body(tokens, expert_ids, gate_numer, gate_weight, up_weight, down_weight):
    tok = tokens.shape[0]
    width = tokens.shape[1]
    groups = lax.axis_size("group")
    members = lax.axis_size(("expert", "hid"))
    local = gate_weight.shape[0]
    experts = groups * local
    flat = expert_ids.reshape(tok * TOPK)
    onehot = (flat[:, None] == jnp.arange(experts, dtype=jnp.int32)[None, :]).astype(jnp.int32)
    before = jnp.cumsum(onehot, axis=0) - onehot
    place = jnp.sum(before * onehot, axis=1)
    target = flat * CAP + place
    slot_ids = jnp.arange(experts * CAP, dtype=jnp.int32)
    scatter_mat = (slot_ids[:, None] == target[None, :]).astype(jnp.bfloat16)
    collect_mat = (target[:, None] == slot_ids[None, :]).astype(jnp.bfloat16)
    copies = jnp.repeat(tokens, TOPK, axis=0)
    outgoing = jnp.dot(scatter_mat, copies, preferred_element_type=jnp.float32).astype(jnp.bfloat16)
    outgoing = outgoing.reshape(groups, local * CAP, width)
    arrived = lax.all_to_all(outgoing, "group", split_axis=0, concat_axis=0, tiled=True)
    partial_value = expert_block(
        lax.all_gather(arrived, ("expert", "hid"), axis=0, tiled=True),
        gate_weight,
        up_weight,
        down_weight,
    )
    partial_value = partial_value.reshape(members, groups, local * CAP, width)
    summed = lax.psum_scatter(
        partial_value.astype(jnp.bfloat16), ("expert", "hid"), scatter_dimension=0, tiled=True
    )
    returned = lax.all_to_all(summed, "group", split_axis=1, concat_axis=1, tiled=True)
    results = returned.reshape(experts * CAP, width)
    values = jnp.dot(collect_mat, results, preferred_element_type=jnp.float32)
    route_w = gate_numer.astype(jnp.float32) * (1.0 / 64.0)
    weighted = values.reshape(tok, TOPK, width) * route_w[:, :, None]
    return jnp.sum(weighted, axis=1).astype(jnp.bfloat16)


def solution(mesh):
    return jax.shard_map(
        body,
        mesh=mesh,
        in_specs=(
            P(("group", "expert", "hid"), None),
            P(("group", "expert", "hid"), None),
            P(("group", "expert", "hid"), None),
            P("group", None, ("expert", "hid")),
            P("group", None, ("expert", "hid")),
            P("group", ("expert", "hid"), None),
        ),
        out_specs=P(("group", "expert", "hid"), None),
        check_vma=False,
    )
```

profile of v0, /device:TPU:0, one launch (start us, length us, event | category | flops | bytes accessed | tf_op | source)
XLA Modules:
  0.0 218.1 jit_solution(17236432761761706072)
XLA Ops:
  6.5 0.0 all-gather.2.cloned.1.call-start
  6.5 0.8 copy.29
  7.3 0.1 eq.57
  7.4 0.1 fusion.20
  7.5 0.2 select_reduce_fusion
  7.7 0.9 broadcast_in_dim.2
  8.6 0.1 reshape.56
  8.7 0.2 convolution_convert_fusion
  8.9 9.7 %all_to_all.10 = bf16[2,16,4096]{2,1,0:T(8,128)(2,1)} all-to-all(bf16[2,16,4096]{2,1,0:T(8,128)(2,1)S(1)} %bitcast.61), channel_id=1, replica_groups=mesh['group'=2,'expert'=4,'hid'=4] {'group'}, dimensions={0} | all-to-all | bytes 524288 | tf_op jit(solution)/shard_map/all_to_all | solution.py:38
  18.6 0.0 all-gather.2.cloned.1.call-update
  18.6 0.0 reduce-scatter.2.cloned.1.call-start
  18.6 51.2 %all-gather.2.cloned.1.call-done = bf16[32,16,4096]{2,1,0:T(8,128)(2,1)} async-done(((bf16[2,16,4096]{2,1,0:T(8,128)(2,1)}), bf16[32,16,4096]{2,1,0:T(8,128)(2,1)}) %all-gather.2.cloned.1.call-update) | async-done | bytes 4194320 | tf_op jit(solution)/shard_map/all_gather | solution.py:40
  69.9 4.5 %copy.32 = bf16[32,16,4096]{2,0,1:T(8,128)(2,1)S(1)} copy(bf16[32,16,4096]{2,1,0:T(8,128)(2,1)} %all-gather.2.cloned.1.call-done) | data formatting | bytes 8388608 | tf_op jit(solution)/shard_map/all_gather | solution.py:40
  74.4 12.0 %fusion.4 = f32[4,32,4,896]{3,1,2,0:T(8,128)S(1)} fusion(bf16[32,4,4,4096]{3,0,2,1:T(8,128)(2,1)S(1)} %bitcast.58, bf16[4,4096,896]{2,1,0:T(8,128)(2,1)} %param.9), kind=kOutput, calls=%fused_computation.4 | convolution fusion | flops 3758096384 | bytes 35389440 | tf_op jit(solution)/shard_map/mlcd,ldf->mlcf/dot_general | solution.py:13
  86.4 13.2 %fusion.12 = bf16[32,4,4,896]{3,0,2,1:T(8,128)(2,1)} fusion(f32[4,32,4,896]{3,1,2,0:T(8,128)S(1)} %fusion.4, bf16[32,4,4,4096]{3,0,2,1:T(8,128)(2,1)S(1)} %bitcast.59, bf16[4,4096,896]{2,1,0:T(8,128)(2,1)} %param.10), kind=kOutput, calls=%fused_computation.11 | convolution fusion | flops 3760848896 | bytes 36306944 | tf_op jit(solution)/shard_map/mlcd,ldf->mlcf/dot_general | solution.py:14
  99.6 16.1 %fusion.9 = bf16[32,4,4,4096]{3,0,2,1:T(8,128)(2,1)} fusion(bf16[32,4,4,896]{3,0,2,1:T(8,128)(2,1)} %fusion.12, bf16[4,896,4096]{2,1,0:T(8,128)(2,1)} %param.11), kind=kOutput, calls=%fused_computation.7 | convolution fusion | flops 3760193536 | bytes 34471936 | tf_op jit(solution)/shard_map/mlcf,lfd->mlcd/dot_general | solution.py:16
  115.7 7.6 %convert_element_type.31 = bf16[16,2,16,4096]{3,1,0,2:T(2,128)(2,1)} reshape(bf16[32,4,4,4096]{3,0,2,1:T(8,128)(2,1)} %fusion.9) | data formatting | bytes 8388608 | tf_op jit(solution)/shard_map/convert_element_type | solution.py:47
  123.4 7.0 %copy.33 = bf16[16,2,16,4096]{3,2,1,0:T(8,128)(2,1)} copy(bf16[16,2,16,4096]{3,1,0,2:T(2,128)(2,1)} %convert_element_type.31) | data formatting | bytes 8388608 | tf_op jit(solution)/shard_map/convert_element_type | solution.py:47
  130.4 0.0 copy-start
  130.4 0.0 reduce-scatter.2.cloned.1.call-update
  130.4 0.1 reduce_sum.21
  130.5 0.1 copy.31
  130.6 71.2 %reduce-scatter.2.cloned.1.call-done = bf16[1,2,16,4096]{3,2,1,0:T(8,128)(2,1)} async-done(((bf16[16,2,16,4096]{3,2,1,0:T(8,128)(2,1)}), bf16[1,2,16,4096]{3,2,1,0:T(8,128)(2,1)}) %reduce-scatter.2.cloned.1.call-update) | async-done | bytes 262160 | tf_op jit(solution)/shard_map/reduce_scatter | solution.py:46
  201.8 3.4 %all-to-all-start.1 = ((bf16[1,2,16,4096]{3,2,0,1:T(8,128)(2,1)}), bf16[1,2,16,4096]{3,2,0,1:T(8,128)(2,1)S(1)}, u32[]{:S(2)}, u32[]{:S(2)}) async-start(bf16[1,2,16,4096]{3,2,0,1:T(8,128)(2,1)} %bitcast.62), calls=%async_computation.2 | async-start | bytes 524288 | tf_op jit(solution)/shard_map/all_to_all | solution.py:49
  205.2 0.0 copy-done
  205.2 5.1 %all-to-all-done.1 = bf16[1,2,16,4096]{3,2,0,1:T(8,128)(2,1)S(1)} async-done(((bf16[1,2,16,4096]{3,2,0,1:T(8,128)(2,1)}), bf16[1,2,16,4096]{3,2,0,1:T(8,128)(2,1)S(1)}, u32[]{:S(2)}, u32[]{:S(2)}) %all-to-all-start.1) | async-done | bytes 262176 | tf_op jit(solution)/shard_map/all_to_all | solution.py:49
  210.4 0.9 fusion.18
  (4 shorter events, 0.1 us)
Async XLA Ops:
  6.5 63.4 %all-gather.2.cloned.1.call-start = ((), (), s32[]{:S(2)}) async-start(), calls=%async_computation.3 | async-start | bytes 4456448 | tf_op jit(solution)/shard_map/all_gather | solution.py:40
  18.6 183.2 %reduce-scatter.2.cloned.1.call-start = ((), (), s32[]{:S(2)}) async-start(), calls=%async_computation.4 | async-start | bytes 4456448 | tf_op jit(solution)/shard_map/reduce_scatter | solution.py:46
  130.4 74.8 %copy-start = (s32[8,2]{0,1:T(2,128)S(1)}, s32[8,2]{0,1:T(2,128)}, u32[]{:S(2)}) copy-start(s32[8,2]{0,1:T(2,128)} %param.8) | copy-start | bytes 196
  201.8 8.6 %all-to-all-start.1 = ((bf16[1,2,16,4096]{3,2,0,1:T(8,128)(2,1)}), bf16[1,2,16,4096]{3,2,0,1:T(8,128)(2,1)S(1)}, u32[]{:S(2)}, u32[]{:S(2)}) async-start(bf16[1,2,16,4096]{3,2,0,1:T(8,128)(2,1)} %bitcast.62), calls=%async_computation.2 | async-start | bytes 524288 | tf_op jit(solution)/shard_map/all_to_all | solution.py:49
Sparse Core Ops, SparseCore 0:
  18.7 51.1 all-gather.1
  130.5 71.1 reduce-scatter.1
where the time goes:
time: 219 us; the launch traced here: 218 us
  waiting for transfers between devices  128 us (58%)
  matrix products  42.4 us (19%)
  local copies, waits for them, and re-layouts  21.1 us (10%)
  between operations  13.5 us (6%)
  blocking collectives  9.71 us (4%)
  starting transfers between devices  3.48 us (2%)
    reduce_scatter x1, waiting for transfers between devices, body(): lax.psum_scatter(partial_value.astype(jnp.bfloat16), ('expert', 'hid'), s...  71.2 us
    all_gather x1, waiting for transfers between devices, body(): lax.all_gather(arrived, ('expert', 'hid'), axis=0, tiled=True)  51.2 us
    dot_general x1, matrix products, expert_block(): jnp.einsum('mlcf,lfd->mlcd', hidden, w_down, preferred_element_type=jnp.f...  16.1 us
    convert_element_type x2, local copies, waits for them, and re-layouts, body(): partial_value.astype(jnp.bfloat16)  14.6 us
    dot_general x1, matrix products, expert_block(): jnp.einsum('mlcd,ldf->mlcf', grid, w_up, preferred_element_type=jnp.float32)  13.2 us
    dot_general x1, matrix products, expert_block(): jnp.einsum('mlcd,ldf->mlcf', grid, w_gate, preferred_element_type=jnp.flo...  12 us
    all_to_all x1, blocking collectives, body(): lax.all_to_all(outgoing, 'group', split_axis=0, concat_axis=0, tiled=True)  9.71 us
    all_to_all x1, waiting for transfers between devices, body(): lax.all_to_all(summed, 'group', split_axis=1, concat_axis=1, tiled=True)  5.14 us
  transfers between devices with their start and end apart: 3, of which 3 were waited for; matrix products, arithmetic and copies ran while one was open for 0% of the time, Pallas kernels for 0%

commit v1 on v0

v1 whole, which is shorter than its diff:
```python
import functools

import jax
import jax.numpy as jnp
from jax import lax
from jax.experimental import pallas as pl
from jax.experimental.pallas import tpu as pltpu
from jax.sharding import PartitionSpec as P

AXES = ("group", "expert", "hid")
LANES = 128
ROW_BLOCK = 256
VMEM = 60 * 1024 * 1024


def tile_of(extent, most):
    return max(t for t in range(LANES, most + 1, LANES) if extent % t == 0)


def ffn_kernel(kt, nt, x_ref, wg, wu, wd, out_ref, gbuf, ubuf, dbuf, acc, hid, gsem, usem, dsem):
    local, width, ff = wg.shape
    nk, nn = width // kt, width // nt
    gslots, dslots = gbuf.shape[0], dbuf.shape[0]
    first = lax.axis_index("group") * local

    def gate_copies(i):
        e, k = i // nk, lax.rem(i, nk)
        s = lax.rem(i, gslots)
        rows = pl.ds(pl.multiple_of(k * kt, kt), kt)
        return (
            pltpu.make_async_copy(wg.at[e, rows, :], gbuf.at[s], gsem.at[s]),
            pltpu.make_async_copy(wu.at[e, rows, :], ubuf.at[s], usem.at[s]),
        )

    def down_copy(i):
        e, n = i // nn, lax.rem(i, nn)
        s = lax.rem(i, dslots)
        cols = pl.ds(pl.multiple_of(n * nt, nt), nt)
        return pltpu.make_async_copy(wd.at[e, :, cols], dbuf.at[s], dsem.at[s])

    def start_gate(i):
        @pl.when(i < local * nk)
        def _():
            for copy in gate_copies(i):
                copy.start()

    def start_down(i):
        @pl.when(i < local * nn)
        def _():
            down_copy(i).start()

    for i in range(min(gslots, local * nk)):
        for copy in gate_copies(jnp.int32(i)):
            copy.start()
    for i in range(min(dslots, local * nn)):
        down_copy(jnp.int32(i)).start()

    route = x_ref[:, width:].astype(jnp.float32)
    lane = lax.broadcasted_iota(jnp.int32, route.shape, 1)

    def expert(e, carry):
        def up(k, carry):
            i = e * nk + k
            s = lax.rem(i, gslots)
            for copy in gate_copies(i):
                copy.wait()
            x = x_ref[:, pl.ds(pl.multiple_of(k * kt, kt), kt)]
            gate = jnp.dot(x, gbuf[s], preferred_element_type=jnp.float32)
            upper = jnp.dot(x, ubuf[s], preferred_element_type=jnp.float32)

            @pl.when(k == 0)
            def _():
                acc[0] = gate
                acc[1] = upper

            @pl.when(k > 0)
            def _():
                acc[0] += gate
                acc[1] += upper

            start_gate(i + gslots)
            return carry

        lax.fori_loop(0, nk, up, 0)
        scale = jnp.sum(jnp.where(lane == first + e, route, 0.0), axis=1, keepdims=True)
        gate = acc[0]
        hid[...] = (gate / (1.0 + jnp.exp(-gate)) * acc[1] * scale).astype(jnp.bfloat16)

        def down(n, carry):
            i = e * nn + n
            s = lax.rem(i, dslots)
            down_copy(i).wait()
            part = jnp.dot(hid[...], dbuf[s], preferred_element_type=jnp.float32)
            cols = pl.ds(pl.multiple_of(n * nt, nt), nt)

            @pl.when(e == 0)
            def _():
                out_ref[:, cols] = part

            @pl.when(e > 0)
            def _():
                out_ref[:, cols] += part

            start_down(i + dslots)
            return carry

        lax.fori_loop(0, nn, down, 0)
        return carry

    lax.fori_loop(0, local, expert, 0)


def ffn(x, wg, wu, wd):
    rows = x.shape[0]
    local, width, ff = wg.shape
    kt, nt = tile_of(width, 512), tile_of(width, 1024)
    gslots, dslots = min(12, local * (width // kt)), min(6, local * (width // nt))
    anywhere = pl.BlockSpec(memory_space=pl.ANY)
    vmem = pl.BlockSpec(memory_space=pltpu.VMEM)
    return pl.pallas_call(
        functools.partial(ffn_kernel, kt, nt),
        out_shape=jax.ShapeDtypeStruct((rows, width), jnp.float32),
        in_specs=[vmem, anywhere, anywhere, anywhere],
        out_specs=vmem,
        scratch_shapes=[
            pltpu.VMEM((gslots, kt, ff), jnp.bfloat16),
            pltpu.VMEM((gslots, kt, ff), jnp.bfloat16),
            pltpu.VMEM((dslots, ff, nt), jnp.bfloat16),
            pltpu.VMEM((2, rows, ff), jnp.float32),
            pltpu.VMEM((rows, ff), jnp.bfloat16),
            pltpu.SemaphoreType.DMA((gslots,)),
            pltpu.SemaphoreType.DMA((gslots,)),
            pltpu.SemaphoreType.DMA((dslots,)),
        ],
        compiler_params=pltpu.CompilerParams(vmem_limit_bytes=VMEM),
        cost_estimate=pl.CostEstimate(
            flops=6 * rows * local * width * ff,
            bytes_accessed=6 * local * width * ff,
            transcendentals=rows * local * ff,
        ),
    )(x, wg, wu, wd)


def pack(tokens, expert_ids, gate_numer, experts):
    lane = jnp.arange(-(-experts // LANES) * LANES, dtype=jnp.int32)
    route = gate_numer.astype(jnp.float32) * (1.0 / 64.0)
    dense = jnp.sum(jnp.where(expert_ids[:, :, None] == lane, route[:, :, None], 0.0), axis=1)
    return jnp.concatenate([tokens, dense.astype(jnp.bfloat16)], axis=1)


def body(tokens, expert_ids, gate_numer, gate_weight, up_weight, down_weight):
    local = gate_weight.shape[0]
    experts = lax.axis_size("group") * local
    packed = pack(tokens, expert_ids, gate_numer, experts)
    x = lax.all_gather(packed, AXES, axis=0, tiled=True)
    rows = x.shape[0]
    if rows > ROW_BLOCK:
        parts = [
            ffn(x[r : r + ROW_BLOCK], gate_weight, up_weight, down_weight).astype(jnp.bfloat16)
            for r in range(0, rows, ROW_BLOCK)
        ]
        total = jnp.concatenate(parts, axis=0)
    else:
        total = ffn(x, gate_weight, up_weight, down_weight).astype(jnp.bfloat16)
    return lax.psum_scatter(total, AXES, scatter_dimension=0, tiled=True)


def solution(mesh):
    return jax.shard_map(
        body,
        mesh=mesh,
        in_specs=(
            P(AXES, None),
            P(AXES, None),
            P(AXES, None),
            P("group", None, ("expert", "hid")),
            P("group", None, ("expert", "hid")),
            P("group", ("expert", "hid"), None),
        ),
        out_specs=P(AXES, None),
        check_vma=False,
    )
```

time: 219 us -> 265 us (1.21)
  waiting for transfers between devices: 128 us -> 196 us
  Pallas kernels: 0 us -> 48.3 us
  matrix products: 42.4 us -> 0 us
  local copies, waits for them, and re-layouts: 21.1 us -> 0 us
  blocking collectives: 9.71 us -> 0 us
  other arithmetic: 0.31 us -> 6.69 us
  starting transfers between devices: 3.48 us -> 0.04 us
    reduce_scatter x1, waiting for transfers between devices: 71.2 us -> 136 us  [body(): return lax.psum_scatter(total, AXES, scatter_dimension=0, tiled=True)]
    pallas_call x0 -> x1, Pallas kernels: none -> 48.3 us  [ffn(): pl.pallas_call(functools.partial(ffn_kernel, kt, nt), out_shape=jax.Shape...]
    dot_general x5 -> x0, matrix products: 42.4 us -> none  [the longest x1 16.1 us: expert_block(): jnp.einsum('mlcf,lfd->mlcd', hidden, w_down, preferred_element_type=jnp.f...]
    convert_element_type x2 -> x0, local copies, waits for them, and re-layouts: 14.6 us -> none  [body(): partial_value.astype(jnp.bfloat16)]
    all_to_all x1 -> x0, blocking collectives: 9.71 us -> none  [body(): lax.all_to_all(outgoing, 'group', split_axis=0, concat_axis=0, tiled=True)]
    all_gather x1, waiting for transfers between devices: 51.2 us -> 60.1 us  [body(): x = lax.all_gather(packed, AXES, axis=0, tiled=True)]
    all_to_all x1 -> x0, waiting for transfers between devices: 5.14 us -> none  [body(): lax.all_to_all(summed, 'group', split_axis=1, concat_axis=1, tiled=True)]
    all_gather x1 -> x0, local copies, waits for them, and re-layouts: 4.49 us -> none  [body(): lax.all_gather(arrived, ('expert', 'hid'), axis=0, tiled=True)]
  transfers between devices with their start and end apart: 3 -> 2, of which waited for: 3 -> 2; matrix products, arithmetic and copies ran while one was open for 0% -> 0% of each run, Pallas kernels for 0% -> 0%
where the time goes in v1:
time: 265 us
  waiting for transfers between devices  196 us (74%)
  Pallas kernels  48.3 us (18%)
  between operations  13.4 us (5%)
  other arithmetic  6.69 us (3%)
    reduce_scatter x1, waiting for transfers between devices, body(): return lax.psum_scatter(total, AXES, scatter_dimension=0, tiled=True)  136 us
    all_gather x1, waiting for transfers between devices, body(): x = lax.all_gather(packed, AXES, axis=0, tiled=True)  60.1 us
    pallas_call x1, Pallas kernels, ffn(): pl.pallas_call(functools.partial(ffn_kernel, kt, nt), out_shape=jax.Shape...  48.3 us
  transfers between devices with their start and end apart: 2, of which 2 were waited for; matrix products, arithmetic and copies ran while one was open for 0% of the time, Pallas kernels for 0%

profile of v1, /device:TPU:0, one launch (start us, length us, event | category | flops | bytes accessed | tf_op | source)
XLA Modules:
  0.0 264.5 jit_solution(4495633008440131492)
XLA Ops:
  6.5 0.0 all-gather.2.cloned.1.call-start
  6.5 0.7 convert_multiply_fusion
  7.2 0.8 select_reduce_fusion
  8.0 1.5 pad_maximum_fusion
  9.4 0.0 all-gather.2.cloned.1.call-update
  9.5 0.0 reduce-scatter.2.cloned.1.call-start
  9.5 60.1 %all-gather.2.cloned.1.call-done.x_ref = bf16[256,4224]{1,0:T(8,128)(2,1)} async-done(((bf16[8,4224]{1,0:T(8,128)(2,1)}), bf16[256,4224]{1,0:T(8,128)(2,1)}) %all-gather.2.cloned.1.call-update) | async-done | bytes 2162704 | tf_op jit(solution)/shard_map/all_gather | solution.py:155
  69.7 48.3 %shard_map.64 = f32[256,4096]{1,0:T(8,128)} custom-call(bf16[256,4224]{1,0:T(8,128)(2,1)} %all-gather.2.cloned.1.call-done.x_ref, bf16[4,4096,896]{2,1,0:T(8,128)(2,1)} %wg.1, bf16[4,4096,896]{2,1,0:T(8,128)(2,1)} %wu.1, bf16[4,896,4096]{2,1,0:T(8,128)(2,1)} %wd.1), custom_call_target="tpu_custom_call" | custom-call | flops 22548578304 | bytes 88080384 | tf_op jit(solution)/shard_map/pallas_call | solution.py:120
  118.0 3.8 %convert_element_type.11 = bf16[256,4096]{1,0:T(8,128)(2,1)} convert(f32[256,4096]{1,0:T(8,128)} %shard_map.64) | non-fusion elementwise | flops 1048576 | bytes 6291456 | tf_op jit(solution)/shard_map/convert_element_type | solution.py:164
  121.8 0.0 reduce-scatter.2.cloned.1.call-update
  121.8 135.8 %reduce-scatter.2.cloned.1.call-done = bf16[8,4096]{1,0:T(8,128)(2,1)} async-done(((bf16[256,4096]{1,0:T(8,128)(2,1)}), bf16[8,4096]{1,0:T(8,128)(2,1)}) %reduce-scatter.2.cloned.1.call-update) | async-done | bytes 65552 | tf_op jit(solution)/shard_map/reduce_scatter | solution.py:165
Async XLA Ops:
  6.5 63.1 %all-gather.2.cloned.1.call-start = ((), (), s32[]{:S(2)}) async-start(), calls=%async_computation.1 | async-start | bytes 2230272 | tf_op jit(solution)/shard_map/all_gather | solution.py:155
  9.5 248.2 %reduce-scatter.2.cloned.1.call-start = ((), (), s32[]{:S(2)}) async-start(), calls=%async_computation.2 | async-start | bytes 2162688 | tf_op jit(solution)/shard_map/reduce_scatter | solution.py:165
Sparse Core Ops, SparseCore 0:
  10.2 59.4 all-gather.1
  122.0 135.6 reduce-scatter.1

commit v2 on v1

--- a/solution.py
+++ b/solution.py
@@ -8,6 +8,7 @@
 from jax.sharding import PartitionSpec as P
 
 AXES = ("group", "expert", "hid")
+MEMBERS = ("expert", "hid")
 LANES = 128
 ROW_BLOCK = 256
 VMEM = 60 * 1024 * 1024
@@ -17,7 +18,7 @@
     return max(t for t in range(LANES, most + 1, LANES) if extent % t == 0)
 
 
-def ffn_kernel(kt, nt, x_ref, wg, wu, wd, out_ref, gbuf, ubuf, dbuf, acc, hid, gsem, usem, dsem):
+def ffn_kernel(kt, nt, x_ref, wg, wu, wd, out_ref, gbuf, ubuf, dbuf, acc, total, hid, gsem, usem, dsem):
     local, width, ff = wg.shape
     nk, nn = width // kt, width // nt
     gslots, dslots = gbuf.shape[0], dbuf.shape[0]
@@ -95,11 +96,18 @@
 
             @pl.when(e == 0)
             def _():
-                out_ref[:, cols] = part
+                total[:, cols] = part
 
-            @pl.when(e > 0)
+            @pl.when((e > 0) & (e < local - 1))
             def _():
-                out_ref[:, cols] += part
+                total[:, cols] += part
+
+            @pl.when((e > 0) & (e == local - 1))
+            def _():
+                out_ref[:, cols] = (total[:, cols] + part).astype(out_ref.dtype)
+
+            if local == 1:
+                out_ref[:, cols] = part.astype(out_ref.dtype)
 
             start_down(i + dslots)
             return carry
@@ -113,13 +121,13 @@
 def ffn(x, wg, wu, wd):
     rows = x.shape[0]
     local, width, ff = wg.shape
-    kt, nt = tile_of(width, 512), tile_of(width, 1024)
-    gslots, dslots = min(12, local * (width // kt)), min(6, local * (width // nt))
+    kt, nt = tile_of(width, 1024), tile_of(width, 1024)
+    gslots, dslots = min(6, local * (width // kt)), min(6, local * (width // nt))
     anywhere = pl.BlockSpec(memory_space=pl.ANY)
     vmem = pl.BlockSpec(memory_space=pltpu.VMEM)
     return pl.pallas_call(
         functools.partial(ffn_kernel, kt, nt),
-        out_shape=jax.ShapeDtypeStruct((rows, width), jnp.float32),
+        out_shape=jax.ShapeDtypeStruct((rows, width), jnp.bfloat16),
         in_specs=[vmem, anywhere, anywhere, anywhere],
         out_specs=vmem,
         scratch_shapes=[
@@ -127,6 +135,7 @@
             pltpu.VMEM((gslots, kt, ff), jnp.bfloat16),
             pltpu.VMEM((dslots, ff, nt), jnp.bfloat16),
             pltpu.VMEM((2, rows, ff), jnp.float32),
+            pltpu.VMEM((rows, width), jnp.float32),
             pltpu.VMEM((rows, ff), jnp.bfloat16),
             pltpu.SemaphoreType.DMA((gslots,)),
             pltpu.SemaphoreType.DMA((gslots,)),
@@ -148,21 +157,29 @@
     return jnp.concatenate([tokens, dense.astype(jnp.bfloat16)], axis=1)
 
 
+def shifted(block, groups, by):
+    return lax.ppermute(block, "group", [(g, (g + by) % groups) for g in range(groups)])
+
+
 def body(tokens, expert_ids, gate_numer, gate_weight, up_weight, down_weight):
     local = gate_weight.shape[0]
     experts = lax.axis_size("group") * local
     packed = pack(tokens, expert_ids, gate_numer, experts)
-    x = lax.all_gather(packed, AXES, axis=0, tiled=True)
+    groups, tok = lax.axis_size("group"), tokens.shape[0]
+    turned = [packed] + [shifted(packed, groups, s) for s in range(1, groups)]
+    x = lax.all_gather(jnp.concatenate(turned, axis=0), MEMBERS, axis=0, tiled=True)
     rows = x.shape[0]
-    if rows > ROW_BLOCK:
-        parts = [
-            ffn(x[r : r + ROW_BLOCK], gate_weight, up_weight, down_weight).astype(jnp.bfloat16)
-            for r in range(0, rows, ROW_BLOCK)
-        ]
-        total = jnp.concatenate(parts, axis=0)
-    else:
-        total = ffn(x, gate_weight, up_weight, down_weight).astype(jnp.bfloat16)
-    return lax.psum_scatter(total, AXES, scatter_dimension=0, tiled=True)
+    parts = [
+        ffn(x[r : r + ROW_BLOCK], gate_weight, up_weight, down_weight)
+        for r in range(0, rows, ROW_BLOCK)
+    ]
+    total = parts[0] if len(parts) == 1 else jnp.concatenate(parts, axis=0)
+    summed = lax.psum_scatter(total, MEMBERS, scatter_dimension=0, tiled=True)
+    mixed = summed[:tok].astype(jnp.float32)
+    for s in range(1, groups):
+        back = shifted(summed[s * tok : (s + 1) * tok], groups, groups - s)
+        mixed = mixed + back.astype(jnp.float32)
+    return mixed.astype(jnp.bfloat16)
 
 
 def solution(mesh):

time: 265 us -> 176 us (0.66)
  waiting for transfers between devices: 196 us -> 109 us
  Pallas kernels: 48.3 us -> 42.7 us
  starting transfers between devices: 0.04 us -> 4.45 us
    reduce_scatter x1, waiting for transfers between devices: 136 us -> 60.6 us  [body(): summed = lax.psum_scatter(total, MEMBERS, scatter_dimension=0, tiled=True)]
    all_gather x1, waiting for transfers between devices: 60.1 us -> 43.4 us  [body(): lax.all_gather(jnp.concatenate(turned, axis=0), MEMBERS, axis=0, tiled=True)]
    pallas_call x1, Pallas kernels: 48.3 us -> 42.7 us  [ffn(): pl.pallas_call(functools.partial(ffn_kernel, kt, nt), out_shape=jax.Shape...]
    ppermute x0 -> x2, waiting for transfers between devices: none -> 5.06 us  [shifted(): lax.ppermute(block, 'group', [(g, (g + by) % groups) for g in range(group...]
    ppermute x0 -> x2, starting transfers between devices: none -> 4.41 us  [shifted(): lax.ppermute(block, 'group', [(g, (g + by) % groups) for g in range(group...]
  transfers between devices with their start and end apart: 2 -> 4, of which waited for: 2 -> 4; matrix products, arithmetic and copies ran while one was open for 0% -> 0% of each run, Pallas kernels for 0% -> 0%
where the time goes in v2:
time: 176 us
  waiting for transfers between devices  109 us (62%)
  Pallas kernels  42.7 us (24%)
  between operations  13.4 us (8%)
  other arithmetic  5.27 us (3%)
  starting transfers between devices  4.45 us (3%)
    reduce_scatter x1, waiting for transfers between devices, body(): summed = lax.psum_scatter(total, MEMBERS, scatter_dimension=0, tiled=True)  60.6 us
    all_gather x1, waiting for transfers between devices, body(): lax.all_gather(jnp.concatenate(turned, axis=0), MEMBERS, axis=0, tiled=True)  43.4 us
    pallas_call x1, Pallas kernels, ffn(): pl.pallas_call(functools.partial(ffn_kernel, kt, nt), out_shape=jax.Shape...  42.7 us
    ppermute x2, waiting for transfers between devices, shifted(): lax.ppermute(block, 'group', [(g, (g + by) % groups) for g in range(group...  5.06 us
    ppermute x2, starting transfers between devices, shifted(): lax.ppermute(block, 'group', [(g, (g + by) % groups) for g in range(group...  4.41 us
  transfers between devices with their start and end apart: 4, of which 4 were waited for; matrix products, arithmetic and copies ran while one was open for 0% of the time, Pallas kernels for 0%

profile of v2, /device:TPU:0, one launch (start us, length us, event | category | flops | bytes accessed | tf_op | source)
XLA Modules:
  0.0 175.7 jit_solution(2546670547997861825)
XLA Ops:
  6.5 0.0 all-gather.2.cloned.1.call-start
  6.5 0.7 convert_multiply_fusion
  7.2 0.8 select_reduce_fusion
  8.0 0.8 pad_maximum_fusion.1
  8.8 2.9 %collective-permute-start = (bf16[8,4224]{1,0:T(8,128)(2,1)S(1)}, bf16[8,4224]{1,0:T(8,128)(2,1)S(1)}, u32[]{:S(2)}, u32[]{:S(2)}) collective-permute-start(bf16[8,4224]{1,0:T(8,128)(2,1)S(1)} %pad_maximum_fusion.1), channel_id=1, source_target_pairs={{0,16},{16,0},{1,17},{17,1},{2,18},{18,2},{3,19},{19,3},{4,20},{20... | collective-permute-start | bytes 202760 | tf_op jit(solution)/shard_map/ppermute | solution.py:161
  11.8 2.3 %collective-permute-done = bf16[8,4224]{1,0:T(8,128)(2,1)S(1)} collective-permute-done((bf16[8,4224]{1,0:T(8,128)(2,1)S(1)}, bf16[8,4224]{1,0:T(8,128)(2,1)S(1)}, u32[]{:S(2)}, u32[]{:S(2)}) %collective-permute-start) | collective-permute-done | bytes 67616 | tf_op jit(solution)/shard_map/ppermute | solution.py:161
  14.0 1.5 pad_maximum_fusion
  15.5 0.0 all-gather.2.cloned.1.call-update
  15.5 0.0 reduce-scatter.2.cloned.1.call-start
  15.6 43.4 %all-gather.2.cloned.1.call-done.x_ref = bf16[256,4224]{1,0:T(8,128)(2,1)} async-done(((bf16[16,4224]{1,0:T(8,128)(2,1)}), bf16[256,4224]{1,0:T(8,128)(2,1)}) %all-gather.2.cloned.1.call-update) | async-done | bytes 2162704 | tf_op jit(solution)/shard_map/all_gather | solution.py:170
  59.0 42.7 %shard_map.64 = bf16[256,4096]{1,0:T(8,128)(2,1)} custom-call(bf16[256,4224]{1,0:T(8,128)(2,1)} %all-gather.2.cloned.1.call-done.x_ref, bf16[4,4096,896]{2,1,0:T(8,128)(2,1)} %wg.1, bf16[4,4096,896]{2,1,0:T(8,128)(2,1)} %wu.1, bf16[4,896,4096]{2,1,0:T(8,128)(2,1)} %wd.1), custom_call_target="tpu_custom_call" | custom-call | flops 22548578304 | bytes 88080384 | tf_op jit(solution)/shard_map/pallas_call | solution.py:128
  101.7 0.0 reduce-scatter.2.cloned.1.call-update
  101.7 60.6 %reduce-scatter.2.cloned.1.call-done = bf16[16,4096]{1,0:T(8,128)(2,1)} async-done(((bf16[256,4096]{1,0:T(8,128)(2,1)}), bf16[16,4096]{1,0:T(8,128)(2,1)}) %reduce-scatter.2.cloned.1.call-update) | async-done | bytes 131088 | tf_op jit(solution)/shard_map/reduce_scatter | solution.py:177
  162.3 0.8 slice.9
  163.1 1.5 collective-permute-start.1
  164.6 2.8 %collective-permute-done.1 = bf16[8,4096]{1,0:T(8,128)(2,1)S(1)} collective-permute-done((bf16[8,4096]{1,0:T(8,128)(2,1)S(1)}, bf16[8,4096]{1,0:T(8,128)(2,1)S(1)}, u32[]{:S(2)}, u32[]{:S(2)}) %collective-permute-start.1) | collective-permute-done | bytes 65568 | tf_op jit(solution)/shard_map/ppermute | solution.py:161
  167.4 1.5 add_convert_fusion
Async XLA Ops:
  6.5 52.4 %all-gather.2.cloned.1.call-start = ((), (), s32[]{:S(2)}) async-start(), calls=%async_computation.1 | async-start | bytes 2297856 | tf_op jit(solution)/shard_map/all_gather | solution.py:170
  8.8 5.2 %collective-permute-start = (bf16[8,4224]{1,0:T(8,128)(2,1)S(1)}, bf16[8,4224]{1,0:T(8,128)(2,1)S(1)}, u32[]{:S(2)}, u32[]{:S(2)}) collective-permute-start(bf16[8,4224]{1,0:T(8,128)(2,1)S(1)} %pad_maximum_fusion.1), channel_id=1, source_target_pairs={{0,16},{16,0},{1,17},{17,1},{2,18},{18,2},{3,19},{19,3},{4,20},{20... | collective-permute-start | bytes 202760 | tf_op jit(solution)/shard_map/ppermute | solution.py:161
  15.5 146.8 %reduce-scatter.2.cloned.1.call-start = ((), (), s32[]{:S(2)}) async-start(), calls=%async_computation.2 | async-start | bytes 2228224 | tf_op jit(solution)/shard_map/reduce_scatter | solution.py:177
  163.1 4.3 %collective-permute-start.1 = (bf16[8,4096]{1,0:T(8,128)(2,1)S(1)}, bf16[8,4096]{1,0:T(8,128)(2,1)S(1)}, u32[]{:S(2)}, u32[]{:S(2)}) collective-permute-start(bf16[8,4096]{1,0:T(8,128)(2,1)S(1)} %slice.9), channel_id=1, source_target_pairs={{0,16},{16,0},{1,17},{17,1},{2,18},{18,2},{3,19},{19,3},{4,20},{20... | collective-permute-start | bytes 196616 | tf_op jit(solution)/shard_map/ppermute | solution.py:161
Sparse Core Ops, SparseCore 0:
  15.7 43.2 all-gather.1
  101.8 60.4 reduce-scatter.1

commit v3 on v2

--- a/solution.py
+++ b/solution.py
@@ -8,7 +8,6 @@
 from jax.sharding import PartitionSpec as P
 
 AXES = ("group", "expert", "hid")
-MEMBERS = ("expert", "hid")
 LANES = 128
 ROW_BLOCK = 256
 VMEM = 60 * 1024 * 1024
@@ -157,29 +156,35 @@
     return jnp.concatenate([tokens, dense.astype(jnp.bfloat16)], axis=1)
 
 
-def shifted(block, groups, by):
-    return lax.ppermute(block, "group", [(g, (g + by) % groups) for g in range(groups)])
+def swapped(block, axis, bit):
+    pairs = [(i, i ^ bit) for i in range(lax.axis_size(axis))]
+    return lax.ppermute(block, axis, pairs)
+
+
+def bits(axis):
+    size = lax.axis_size(axis)
+    return [1 << b for b in reversed(range(size.bit_length() - 1))]
 
 
 def body(tokens, expert_ids, gate_numer, gate_weight, up_weight, down_weight):
     local = gate_weight.shape[0]
     experts = lax.axis_size("group") * local
     packed = pack(tokens, expert_ids, gate_numer, experts)
-    groups, tok = lax.axis_size("group"), tokens.shape[0]
-    turned = [packed] + [shifted(packed, groups, s) for s in range(1, groups)]
-    x = lax.all_gather(jnp.concatenate(turned, axis=0), MEMBERS, axis=0, tiled=True)
+    steps = [(axis, bit) for axis in ("expert", "group", "hid") for bit in bits(axis)]
+    x = packed
+    for axis, bit in steps:
+        x = jnp.concatenate([x, swapped(x, axis, bit)], axis=0)
     rows = x.shape[0]
     parts = [
         ffn(x[r : r + ROW_BLOCK], gate_weight, up_weight, down_weight)
         for r in range(0, rows, ROW_BLOCK)
     ]
     total = parts[0] if len(parts) == 1 else jnp.concatenate(parts, axis=0)
-    summed = lax.psum_scatter(total, MEMBERS, scatter_dimension=0, tiled=True)
-    mixed = summed[:tok].astype(jnp.float32)
-    for s in range(1, groups):
-        back = shifted(summed[s * tok : (s + 1) * tok], groups, groups - s)
-        mixed = mixed + back.astype(jnp.float32)
-    return mixed.astype(jnp.bfloat16)
+    for axis, bit in reversed(steps):
+        half = total.shape[0] // 2
+        back = swapped(total[half:], axis, bit)
+        total = (total[:half].astype(jnp.float32) + back.astype(jnp.float32)).astype(jnp.bfloat16)
+    return total
 
 
 def solution(mesh):

time: 176 us -> 123 us (0.70)
  waiting for transfers between devices: 109 us -> 50.8 us
  starting transfers between devices: 4.45 us -> 20.1 us
  between operations: 13.4 us -> 0.12 us
  local copies, waits for them, and re-layouts: 0.84 us -> 3.21 us
    reduce_scatter x1 -> x0, waiting for transfers between devices: 60.6 us -> none  [body(): summed = lax.psum_scatter(total, MEMBERS, scatter_dimension=0, tiled=True)]
    ppermute x2 -> x10, waiting for transfers between devices: 5.06 us -> 50.8 us  [swapped(): return lax.ppermute(block, axis, pairs)]
    all_gather x1 -> x0, waiting for transfers between devices: 43.4 us -> none  [body(): lax.all_gather(jnp.concatenate(turned, axis=0), MEMBERS, axis=0, tiled=True)]
    ppermute x2 -> x10, starting transfers between devices: 4.41 us -> 20.1 us  [swapped(): return lax.ppermute(block, axis, pairs)]
  transfers between devices with their start and end apart: 4 -> 10, of which waited for: 4 -> 10; matrix products, arithmetic and copies ran while one was open for 0% -> 0% of each run, Pallas kernels for 0% -> 0%
where the time goes in v3:
time: 123 us
  waiting for transfers between devices  50.8 us (41%)
  Pallas kernels  42.7 us (35%)
  starting transfers between devices  20.1 us (16%)
  other arithmetic  6 us (5%)
  local copies, waits for them, and re-layouts  3.21 us (3%)
    ppermute x10, waiting for transfers between devices, swapped(): return lax.ppermute(block, axis, pairs)  50.8 us
    pallas_call x1, Pallas kernels, ffn(): pl.pallas_call(functools.partial(ffn_kernel, kt, nt), out_shape=jax.Shape...  42.7 us
    ppermute x10, starting transfers between devices, swapped(): return lax.ppermute(block, axis, pairs)  20.1 us
    concatenate x3, other arithmetic, body(): x = jnp.concatenate([x, swapped(x, axis, bit)], axis=0)  2.59 us
  transfers between devices with their start and end apart: 10, of which 10 were waited for; matrix products, arithmetic and copies ran while one was open for 0% of the time, Pallas kernels for 0%

profile of v3, /device:TPU:0, one launch (start us, length us, event | category | flops | bytes accessed | tf_op | source)
XLA Modules:
  0.0 122.9 jit_solution(18287657884336327336)
XLA Ops:
  0.0 0.7 convert_multiply_fusion
  0.7 0.8 select_reduce_fusion
  1.4 0.9 constant_dynamic-update-slice_fusion.4
  2.3 4.1 %collective-permute-start = (bf16[8,4224]{1,0:T(8,128)(2,1)S(1)}, bf16[8,4224]{1,0:T(8,128)(2,1)S(1)}, u32[]{:S(2)}, u32[]{:S(2)}) collective-permute-start(bf16[8,4224]{1,0:T(8,128)(2,1)S(1)} %get-tuple-element.14), channel_id=1, source_target_pairs={{0,8},{4,12},{8,0},{12,4},{1,9},{5,13},{9,1},{13,5},{2,10},{6,14},... | collective-permute-start | bytes 202760 | tf_op jit(solution)/shard_map/ppermute | solution.py:161
  6.4 3.7 %collective-permute-done = bf16[8,4224]{1,0:T(8,128)(2,1)S(1)} collective-permute-done((bf16[8,4224]{1,0:T(8,128)(2,1)S(1)}, bf16[8,4224]{1,0:T(8,128)(2,1)S(1)}, u32[]{:S(2)}, u32[]{:S(2)}) %collective-permute-start) | collective-permute-done | bytes 67616 | tf_op jit(solution)/shard_map/ppermute | solution.py:161
  10.1 0.9 pad_maximum_fusion.2
  11.0 0.7 collective-permute-start.1
  11.6 4.4 %collective-permute-done.1 = bf16[16,4224]{1,0:T(8,128)(2,1)S(1)} collective-permute-done((bf16[16,4224]{1,0:T(8,128)(2,1)S(1)}, bf16[16,4224]{1,0:T(8,128)(2,1)S(1)}, u32[]{:S(2)}, u32[]{:S(2)}) %collective-permute-start.1) | collective-permute-done | bytes 135200 | tf_op jit(solution)/shard_map/ppermute | solution.py:161
  16.0 0.9 pad_maximum_fusion.1
  16.9 1.8 %collective-permute-start.2 = (bf16[32,4224]{1,0:T(8,128)(2,1)S(1)}, bf16[32,4224]{1,0:T(8,128)(2,1)S(1)}, u32[]{:S(2)}, u32[]{:S(2)}) collective-permute-start(bf16[32,4224]{1,0:T(8,128)(2,1)S(1)} %pad_maximum_fusion.1), channel_id=1, source_target_pairs={{0,16},{16,0},{1,17},{17,1},{2,18},{18,2},{3,19},{19,3},{4,20},{20... | collective-permute-start | bytes 811016 | tf_op jit(solution)/shard_map/ppermute | solution.py:161
  18.7 4.7 %collective-permute-done.2 = bf16[32,4224]{1,0:T(8,128)(2,1)S(1)} collective-permute-done((bf16[32,4224]{1,0:T(8,128)(2,1)S(1)}, bf16[32,4224]{1,0:T(8,128)(2,1)S(1)}, u32[]{:S(2)}, u32[]{:S(2)}) %collective-permute-start.2) | collective-permute-done | bytes 270368 | tf_op jit(solution)/shard_map/ppermute | solution.py:161
  23.4 0.9 pad_maximum_fusion
  24.3 1.8 %collective-permute-start.3 = (bf16[64,4224]{1,0:T(8,128)(2,1)S(1)}, bf16[64,4224]{1,0:T(8,128)(2,1)S(1)}, u32[]{:S(2)}, u32[]{:S(2)}) collective-permute-start(bf16[64,4224]{1,0:T(8,128)(2,1)S(1)} %pad_maximum_fusion), channel_id=1, source_target_pairs={{0,2},{1,3},{2,0},{3,1},{4,6},{5,7},{6,4},{7,5},{8,10},{9,11},{10,... | collective-permute-start | bytes 1622024 | tf_op jit(solution)/shard_map/ppermute | solution.py:161
  26.1 8.5 %collective-permute-done.3 = bf16[64,4224]{1,0:T(8,128)(2,1)S(1)} collective-permute-done((bf16[64,4224]{1,0:T(8,128)(2,1)S(1)}, bf16[64,4224]{1,0:T(8,128)(2,1)S(1)}, u32[]{:S(2)}, u32[]{:S(2)}) %collective-permute-start.3) | collective-permute-done | bytes 540704 | tf_op jit(solution)/shard_map/ppermute | solution.py:161
  34.9 2.7 %collective-permute-done.4 = bf16[128,4224]{1,0:T(8,128)(2,1)S(1)} collective-permute-done((bf16[128,4224]{1,0:T(8,128)(2,1)S(1)}, bf16[128,4224]{1,0:T(8,128)(2,1)S(1)}, u32[]{:S(2)}, u32[]{:S(2)}) %collective-permute-start.4) | collective-permute-done | bytes 1081376 | tf_op jit(solution)/shard_map/ppermute | solution.py:161
  37.6 0.1 constant_dynamic-update-slice_fusion.5.x_ref
  37.7 1.3 %copy-done.1 = bf16[256,4224]{1,0:T(8,128)(2,1)} copy-done((bf16[256,4224]{1,0:T(8,128)(2,1)}, bf16[256,4224]{1,0:T(8,128)(2,1)S(1)}, u32[]{:S(2)}) %copy-start.1) | copy-done | bytes 2162712
  39.0 42.7 %shard_map.64 = bf16[256,4096]{1,0:T(8,128)(2,1)} custom-call(bf16[256,4224]{1,0:T(8,128)(2,1)} %copy-done.1, bf16[4,4096,896]{2,1,0:T(8,128)(2,1)} %wg.1, bf16[4,4096,896]{2,1,0:T(8,128)(2,1)} %wu.1, bf16[4,896,4096]{2,1,0:T(8,128)(2,1)} %wd.1), custom_call_target="tpu_custom_call" | custom-call | flops 22548578304 | bytes 88080384 | tf_op jit(solution)/shard_map/pallas_call | solution.py:127
  81.8 1.4 %slice.41 = bf16[128,4096]{1,0:T(8,128)(2,1)S(1)} slice(bf16[256,4096]{1,0:T(8,128)(2,1)} %shard_map.64), slice={[128:256], [0:4096]} | slice | bytes 2097152 | tf_op jit(solution)/shard_map/slice | solution.py:185
  83.2 0.2 collective-permute-start.5
  83.4 2.5 %collective-permute-done.5 = bf16[128,4096]{1,0:T(8,128)(2,1)S(1)} collective-permute-done((bf16[128,4096]{1,0:T(8,128)(2,1)S(1)}, bf16[128,4096]{1,0:T(8,128)(2,1)S(1)}, u32[]{:S(2)}, u32[]{:S(2)}) %collective-permute-start.5) | collective-permute-done | bytes 1048608 | tf_op jit(solution)/shard_map/ppermute | solution.py:161
  85.9 0.2 add_convert_fusion
  86.2 1.6 %collective-permute-start.6 = (bf16[64,4096]{1,0:T(8,128)(2,1)S(1)}, bf16[64,4096]{1,0:T(8,128)(2,1)S(1)}, u32[]{:S(2)}, u32[]{:S(2)}) collective-permute-start(bf16[64,4096]{1,0:T(8,128)(2,1)S(1)} %slice.43), channel_id=1, source_target_pairs={{0,2},{1,3},{2,0},{3,1},{4,6},{5,7},{6,4},{7,5},{8,10},{9,11},{10,... | collective-permute-start | bytes 1572872 | tf_op jit(solution)/shard_map/ppermute | solution.py:161
  87.8 12.4 %collective-permute-done.6 = bf16[64,4096]{1,0:T(8,128)(2,1)S(1)} collective-permute-done((bf16[64,4096]{1,0:T(8,128)(2,1)S(1)}, bf16[64,4096]{1,0:T(8,128)(2,1)S(1)}, u32[]{:S(2)}, u32[]{:S(2)}) %collective-permute-start.6) | collective-permute-done | bytes 524320 | tf_op jit(solution)/shard_map/ppermute | solution.py:161
  100.3 0.1 add_convert_fusion.1
  100.4 1.6 %collective-permute-start.7 = (bf16[32,4096]{1,0:T(8,128)(2,1)S(1)}, bf16[32,4096]{1,0:T(8,128)(2,1)S(1)}, u32[]{:S(2)}, u32[]{:S(2)}) collective-permute-start(bf16[32,4096]{1,0:T(8,128)(2,1)S(1)} %slice.45), channel_id=1, source_target_pairs={{0,16},{16,0},{1,17},{17,1},{2,18},{18,2},{3,19},{19,3},{4,20},{20... | collective-permute-start | bytes 786440 | tf_op jit(solution)/shard_map/ppermute | solution.py:161
  102.0 6.0 %collective-permute-done.7 = bf16[32,4096]{1,0:T(8,128)(2,1)S(1)} collective-permute-done((bf16[32,4096]{1,0:T(8,128)(2,1)S(1)}, bf16[32,4096]{1,0:T(8,128)(2,1)S(1)}, u32[]{:S(2)}, u32[]{:S(2)}) %collective-permute-start.7) | collective-permute-done | bytes 262176 | tf_op jit(solution)/shard_map/ppermute | solution.py:161
  108.1 2.3 %collective-permute-start.8 = (bf16[16,4096]{1,0:T(8,128)(2,1)S(1)}, bf16[16,4096]{1,0:T(8,128)(2,1)S(1)}, u32[]{:S(2)}, u32[]{:S(2)}) collective-permute-start(bf16[16,4096]{1,0:T(8,128)(2,1)S(1)} %slice.47), channel_id=1, source_target_pairs={{0,4},{4,0},{8,12},{12,8},{1,5},{5,1},{9,13},{13,9},{2,6},{6,2},{1... | collective-permute-start | bytes 393224 | tf_op jit(solution)/shard_map/ppermute | solution.py:161
  110.4 2.9 %collective-permute-done.8 = bf16[16,4096]{1,0:T(8,128)(2,1)S(1)} collective-permute-done((bf16[16,4096]{1,0:T(8,128)(2,1)S(1)}, bf16[16,4096]{1,0:T(8,128)(2,1)S(1)}, u32[]{:S(2)}, u32[]{:S(2)}) %collective-permute-start.8) | collective-permute-done | bytes 131104 | tf_op jit(solution)/shard_map/ppermute | solution.py:161
  113.4 6.0 %collective-permute-start.9 = (bf16[8,4096]{1,0:T(8,128)(2,1)S(1)}, bf16[8,4096]{1,0:T(8,128)(2,1)S(1)}, u32[]{:S(2)}, u32[]{:S(2)}) collective-permute-start(bf16[8,4096]{1,0:T(8,128)(2,1)S(1)} %slice.49), channel_id=1, source_target_pairs={{0,8},{4,12},{8,0},{12,4},{1,9},{5,13},{9,1},{13,5},{2,10},{6,14},... | collective-permute-start | bytes 196616 | tf_op jit(solution)/shard_map/ppermute | solution.py:161
  119.5 2.8 %collective-permute-done.9 = bf16[8,4096]{1,0:T(8,128)(2,1)S(1)} collective-permute-done((bf16[8,4096]{1,0:T(8,128)(2,1)S(1)}, bf16[8,4096]{1,0:T(8,128)(2,1)S(1)}, u32[]{:S(2)}, u32[]{:S(2)}) %collective-permute-start.9) | collective-permute-done | bytes 65568 | tf_op jit(solution)/shard_map/ppermute | solution.py:161
  122.3 0.6 add_convert_fusion.4
  (14 shorter events, 0.5 us)
Async XLA Ops:
  2.3 7.8 %collective-permute-start = (bf16[8,4224]{1,0:T(8,128)(2,1)S(1)}, bf16[8,4224]{1,0:T(8,128)(2,1)S(1)}, u32[]{:S(2)}, u32[]{:S(2)}) collective-permute-start(bf16[8,4224]{1,0:T(8,128)(2,1)S(1)} %get-tuple-element.14), channel_id=1, source_target_pairs={{0,8},{4,12},{8,0},{12,4},{1,9},{5,13},{9,1},{13,5},{2,10},{6,14},... | collective-permute-start | bytes 202760 | tf_op jit(solution)/shard_map/ppermute | solution.py:161
  11.0 5.1 %collective-permute-start.1 = (bf16[16,4224]{1,0:T(8,128)(2,1)S(1)}, bf16[16,4224]{1,0:T(8,128)(2,1)S(1)}, u32[]{:S(2)}, u32[]{:S(2)}) collective-permute-start(bf16[16,4224]{1,0:T(8,128)(2,1)S(1)} %pad_maximum_fusion.2), channel_id=1, source_target_pairs={{0,4},{4,0},{8,12},{12,8},{1,5},{5,1},{9,13},{13,9},{2,6},{6,2},{1... | collective-permute-start | bytes 405512 | tf_op jit(solution)/shard_map/ppermute | solution.py:161
  16.9 6.5 %collective-permute-start.2 = (bf16[32,4224]{1,0:T(8,128)(2,1)S(1)}, bf16[32,4224]{1,0:T(8,128)(2,1)S(1)}, u32[]{:S(2)}, u32[]{:S(2)}) collective-permute-start(bf16[32,4224]{1,0:T(8,128)(2,1)S(1)} %pad_maximum_fusion.1), channel_id=1, source_target_pairs={{0,16},{16,0},{1,17},{17,1},{2,18},{18,2},{3,19},{19,3},{4,20},{20... | collective-permute-start | bytes 811016 | tf_op jit(solution)/shard_map/ppermute | solution.py:161
  24.3 10.3 %collective-permute-start.3 = (bf16[64,4224]{1,0:T(8,128)(2,1)S(1)}, bf16[64,4224]{1,0:T(8,128)(2,1)S(1)}, u32[]{:S(2)}, u32[]{:S(2)}) collective-permute-start(bf16[64,4224]{1,0:T(8,128)(2,1)S(1)} %pad_maximum_fusion), channel_id=1, source_target_pairs={{0,2},{1,3},{2,0},{3,1},{4,6},{5,7},{6,4},{7,5},{8,10},{9,11},{10,... | collective-permute-start | bytes 1622024 | tf_op jit(solution)/shard_map/ppermute | solution.py:161
  34.8 2.8 %collective-permute-start.4 = (bf16[128,4224]{1,0:T(8,128)(2,1)S(1)}, bf16[128,4224]{1,0:T(8,128)(2,1)S(1)}, u32[]{:S(2)}, u32[]{:S(2)}) collective-permute-start(bf16[128,4224]{1,0:T(8,128)(2,1)S(1)} %get-tuple-element.5), channel_id=1, source_target_pairs={{0,1},{1,0},{2,3},{3,2},{4,5},{5,4},{6,7},{7,6},{8,9},{9,8},{10,11... | collective-permute-start | bytes 3244040 | tf_op jit(solution)/shard_map/ppermute | solution.py:161
  37.7 1.4 %copy-start.1 = (bf16[256,4224]{1,0:T(8,128)(2,1)}, bf16[256,4224]{1,0:T(8,128)(2,1)S(1)}, u32[]{:S(2)}) copy-start(bf16[256,4224]{1,0:T(8,128)(2,1)S(1)} %constant_dynamic-update-slice_fusion.5.x_ref) | copy-start | bytes 6488068
  81.8 4.2 %copy-start = (bf16[256,4096]{1,0:T(8,128)(2,1)S(1)}, bf16[256,4096]{1,0:T(8,128)(2,1)}, u32[]{:S(2)}) copy-start(bf16[256,4096]{1,0:T(8,128)(2,1)} %shard_map.64) | copy-start | bytes 6291460
  83.2 2.7 %collective-permute-start.5 = (bf16[128,4096]{1,0:T(8,128)(2,1)S(1)}, bf16[128,4096]{1,0:T(8,128)(2,1)S(1)}, u32[]{:S(2)}, u32[]{:S(2)}) collective-permute-start(bf16[128,4096]{1,0:T(8,128)(2,1)S(1)} %slice.41), channel_id=1, source_target_pairs={{0,1},{1,0},{2,3},{3,2},{4,5},{5,4},{6,7},{7,6},{8,9},{9,8},{10,11... | collective-permute-start | bytes 3145736 | tf_op jit(solution)/shard_map/ppermute | solution.py:161
  86.2 14.0 %collective-permute-start.6 = (bf16[64,4096]{1,0:T(8,128)(2,1)S(1)}, bf16[64,4096]{1,0:T(8,128)(2,1)S(1)}, u32[]{:S(2)}, u32[]{:S(2)}) collective-permute-start(bf16[64,4096]{1,0:T(8,128)(2,1)S(1)} %slice.43), channel_id=1, source_target_pairs={{0,2},{1,3},{2,0},{3,1},{4,6},{5,7},{6,4},{7,5},{8,10},{9,11},{10,... | collective-permute-start | bytes 1572872 | tf_op jit(solution)/shard_map/ppermute | solution.py:161
  100.4 7.6 %collective-permute-start.7 = (bf16[32,4096]{1,0:T(8,128)(2,1)S(1)}, bf16[32,4096]{1,0:T(8,128)(2,1)S(1)}, u32[]{:S(2)}, u32[]{:S(2)}) collective-permute-start(bf16[32,4096]{1,0:T(8,128)(2,1)S(1)} %slice.45), channel_id=1, source_target_pairs={{0,16},{16,0},{1,17},{17,1},{2,18},{18,2},{3,19},{19,3},{4,20},{20... | collective-permute-start | bytes 786440 | tf_op jit(solution)/shard_map/ppermute | solution.py:161
  108.1 5.3 %collective-permute-start.8 = (bf16[16,4096]{1,0:T(8,128)(2,1)S(1)}, bf16[16,4096]{1,0:T(8,128)(2,1)S(1)}, u32[]{:S(2)}, u32[]{:S(2)}) collective-permute-start(bf16[16,4096]{1,0:T(8,128)(2,1)S(1)} %slice.47), channel_id=1, source_target_pairs={{0,4},{4,0},{8,12},{12,8},{1,5},{5,1},{9,13},{13,9},{2,6},{6,2},{1... | collective-permute-start | bytes 393224 | tf_op jit(solution)/shard_map/ppermute | solution.py:161
  113.4 8.8 %collective-permute-start.9 = (bf16[8,4096]{1,0:T(8,128)(2,1)S(1)}, bf16[8,4096]{1,0:T(8,128)(2,1)S(1)}, u32[]{:S(2)}, u32[]{:S(2)}) collective-permute-start(bf16[8,4096]{1,0:T(8,128)(2,1)S(1)} %slice.49), channel_id=1, source_target_pairs={{0,8},{4,12},{8,0},{12,4},{1,9},{5,13},{9,1},{13,5},{2,10},{6,14},... | collective-permute-start | bytes 196616 | tf_op jit(solution)/shard_map/ppermute | solution.py:161
